TPU v7x, 32 devices: a whole 2x2x4 slice. The times are simulated.
32 devices in a mesh: rows: 8 (over y, x, core), fields: 4 (over z).
Axes of the slice: x: 2, y: 2, z: 4, core: 2. Of those that a mesh axis runs over, the one named last changes fastest.
Arguments:
- deviation: float32 [64, 3, 128, 2048], P('fields', None, 'rows'), may hold values from -5.5 to 5.5
- seeds: int32 [64], P('fields'), may hold values from 0 to 1048575
- velocity: float32 [2, 128, 2048], P(None, 'rows'), may hold values from -5.5 to 5.5
- forcing: float32 [2, 128, 2048], P(None, 'rows'), may hold values from -6 to 6
Outputs:
- new_deviation: float32 [64, 3, 128, 2048], P('fields', None, 'rows')
- new_velocity: float32 [2, 128, 2048], P(None, 'rows')
All inputs are finite; a program needn't handle non-finite values. Where the computation divides by a largest or mean magnitude, that divisor is 1e-20 or more.
Results may differ from a plain program's by a relative error of at most 0.0003.
Values sent between devices are 32-bit elements; how exact they have to be, the bound alone decides.
A program may use at most 64 MiB of HBM per device.

v0:
```python
import jax
import jax.numpy as jnp
from jax import lax
from jax.sharding import PartitionSpec as P

FIELDS = 64
SWEEPS = 8
STEPS = 2


G_COEF = 4.0
ALPHA = 0.05
LMAX2 = 20.0
LAMBDA = 1.0
DT = 0.2
SIGMA = 1.0


def with_halo(cells, sides, width):
    for axis, dim in sides:
        count = lax.axis_size(axis)
        head = lax.slice_in_dim(cells, 0, width, axis=dim)
        tail = lax.slice_in_dim(cells, cells.shape[dim] - width, cells.shape[dim], axis=dim)
        cells = jnp.concatenate(
            [
                lax.ppermute(tail, axis, [(i, (i + 1) % count) for i in range(count)]),
                cells,
                lax.ppermute(head, axis, [((i + 1) % count, i) for i in range(count)]),
            ],
            axis=dim,
        )
    return cells


def ddx(values):
    return (jnp.roll(values, -1, axis=-1) - jnp.roll(values, 1, axis=-1)) * 0.5


def ddy(values):
    return (values[..., 2:, :] - values[..., :-2, :]) * 0.5


def divergence(tensor):
    fx = ddx(tensor[0, 1:-1]) + ddy(tensor[1])
    fy = ddx(tensor[1, 1:-1]) + ddy(tensor[2])
    return jnp.stack([fx, fy])


def relax(padded, rhs):
    middle = padded[:, 1:-1]
    beside_all = (
        padded[:, 2:]
        + padded[:, :-2]
        + jnp.roll(middle, -1, axis=-1)
        + jnp.roll(middle, 1, axis=-1)
    )
    return (rhs + beside_all) / (ALPHA + 4.0)


def scramble(hashed):
    hashed = jnp.bitwise_xor(hashed, lax.shift_right_logical(hashed, jnp.int32(16)))
    hashed = hashed * jnp.int32(73244475)
    hashed = jnp.bitwise_xor(hashed, lax.shift_right_logical(hashed, jnp.int32(16)))
    hashed = hashed * jnp.int32(73244475)
    hashed = jnp.bitwise_xor(hashed, lax.shift_right_logical(hashed, jnp.int32(16)))
    return hashed


def make_noise(seed_block, step, row_start, row_count, width):
    row_ids = row_start + jnp.arange(row_count, dtype=jnp.int32)
    cell_ids = row_ids[:, None] * jnp.int32(width) + jnp.arange(width, dtype=jnp.int32)[None, :]
    comps = jnp.arange(3, dtype=jnp.int32)
    hashed = (
        seed_block[:, None, None, None] * jnp.int32(2654435)
        + ((3 * step + comps) * 97531)[None, :, None, None]
        + cell_ids[None, None]
    )
    hashed = scramble(hashed)
    return (jnp.bitwise_and(hashed, jnp.int32(65535)).astype(jnp.float32) - 32767.5) / 18918.6


def advance(extended, seed_block, speed_x, speed_y, grads, dt, step, row_start):
    inner = extended[:, :, 1:-1]
    west = jnp.roll(inner, 1, axis=-1)
    east = jnp.roll(inner, -1, axis=-1)
    south = extended[:, :, :-2]
    north = extended[:, :, 2:]
    advect = (
        jnp.maximum(speed_x, 0.0) * (inner - west)
        + jnp.minimum(speed_x, 0.0) * (east - inner)
        + jnp.maximum(speed_y, 0.0) * (inner - south)
        + jnp.minimum(speed_y, 0.0) * (north - inner)
    )
    lxx, lxy, lyx, lyy = grads
    comp_a, comp_b, comp_c = (inner[:, 0], inner[:, 1], inner[:, 2])
    stretch = jnp.stack(
        [
            2.0 * lxx + 2.0 * (lxx * comp_a + lxy * comp_b),
            lxy + lyx + lxx * comp_b + lxy * comp_c + lyx * comp_a + lyy * comp_b,
            2.0 * lyy + 2.0 * (lyx * comp_b + lyy * comp_c),
        ],
        axis=1,
    )
    spring = 1.0 + (2.0 + comp_a + comp_c) / LMAX2
    noise = make_noise(seed_block, step, row_start, inner.shape[2], inner.shape[3])
    return (
        inner
        + dt * (stretch - advect - spring[:, None] * inner / LAMBDA)
        + jnp.sqrt(dt) * SIGMA * noise
    )


def body(deviation, seeds, velocity, forcing):
    row_count = deviation.shape[2]
    row_start = lax.axis_index("rows") * row_count
    field_now = deviation
    speed_now = velocity
    for step in range(STEPS):
        extended = with_halo(field_now, (("rows", 2),), 1)
        spring = 1.0 + (2.0 + extended[:, 0] + extended[:, 2]) / LMAX2
        local_total = jnp.sum(spring[:, None] * extended, axis=0)
        stress = G_COEF / FIELDS * lax.psum(local_total, "fields")
        force = divergence(stress)
        rhs = forcing + force
        for sweep in range(SWEEPS):
            padded = with_halo(speed_now, (("rows", 1),), 1)
            speed_now = relax(padded, rhs)
        rim = with_halo(speed_now, (("rows", 1),), 1)
        grads = (ddx(speed_now[0]), ddy(rim[0]), ddx(speed_now[1]), ddy(rim[1]))
        largest = lax.pmax(jnp.max(jnp.abs(speed_now[0]) + jnp.abs(speed_now[1])), "rows")
        dt = DT / (1.0 + largest)
        field_now = advance(extended, seeds, speed_now[0], speed_now[1], grads, dt, step, row_start)
    return (field_now, speed_now)


def solution(mesh):
    return jax.shard_map(
        body,
        mesh=mesh,
        in_specs=(
            P("fields", None, "rows", None),
            P("fields"),
            P(None, "rows", None),
            P(None, "rows", None),
        ),
        out_specs=(P("fields", None, "rows", None), P(None, "rows", None)),
        check_vma=False,
    )
```

profile of v0, /device:TPU:0, one launch (start us, length us, event | category | flops | bytes accessed | tf_op | source)
XLA Modules:
  0.0 288.5 jit_solution(1014974560888610325)
XLA Ops:
  7.2 6.5 %copy.53 = f32[16,3,16,2048]{3,0,2,1:T(8,128)S(1)} copy(f32[16,3,16,2048]{3,2,1,0:T(8,128)} %param.4) | data formatting | bytes 12582912 | tf_op args[0]
  15.2 2.9 collective-permute-start.1
  20.0 6.7 %fusion.158 = (f32[16,3,16,2047]{3,0,2,1:T(8,128)}, f32[16,3,16,2047]{3,0,2,1:T(8,128)}) fusion(f32[16,3,16,2048]{3,0,2,1:T(8,128)S(1)} %copy.53), kind=kLoop, calls=%fused_computation.302 | loop fusion | bytes 25153536 | tf_op jit(solution)/shard_map/jit(_roll_static)/slice | solution.py:85
  29.0 6.4 %constant_dynamic-update-slice_fusion.1 = f32[16,3,18,2048]{3,0,2,1:T(8,128)S(1)} fusion(f32[16,3,18,2048]{3,0,2,1:T(8,128)S(1)} %constant_dynamic-update-slice_fusion.2, f32[16,3,16,2048]{3,2,1,0:T(8,128)} %param.4), kind=kLoop, calls=%fused_computation.281 | loop fusion | bytes 12582912
  37.1 2.5 multiply_reduce_fusion.1
  39.8 40.6 %all-reduce.3.cloned.1.call-done = f32[3,18,2048]{2,1,0:T(8,128)} async-done(((f32[3,18,2048]{2,1,0:T(8,128)}), f32[3,18,2048]{2,1,0:T(8,128)}) %all-reduce.3.cloned.1.call-update) | async-done | bytes 442384 | tf_op jit(solution)/shard_map/psum | solution.py:122
  86.2 2.6 collective-permute-done.5
  90.6 2.7 collective-permute-done.7
  95.1 2.7 collective-permute-done.9
  99.6 2.7 collective-permute-done.11
  104.1 2.7 collective-permute-done.13
  108.6 2.9 %collective-permute-done.15 = f32[2,1,2048]{2,1,0:T(1,128)S(1)} collective-permute-done((f32[2,1,2048]{2,1,0:T(1,128)S(1)}, f32[2,1,2048]{2,1,0:T(1,128)S(1)}, u32[]{:S(2)}, u32[]{:S(2)}) %collective-permute-start.15) | collective-permute-done | bytes 16416 | tf_op jit(solution)/shard_map/ppermute | solution.py:26
  113.3 2.7 collective-permute-done.17
  118.5 14.6 %pmax.14 = f32[]{:T(128)} all-reduce(f32[]{:T(128)} %get-tuple-element.104), channel_id=1, replica_groups=mesh['rows'=8,'fields'=4] {'rows'}, use_global_device_ids=true, to_apply=%region_3.4 | all-reduce | flops 1 | bytes 8 | tf_op jit(solution)/shard_map/pmax | solution.py:130
  134.4 3.8 %multiply_add_fusion.5 = (f32[16,1,16,2048]{3,0,2,1:T(8,128)S(1)}, f32[16,1,16,2048]{3,0,2,1:T(8,128)S(1)}, f32[16,1,16,2048]{3,0,2,1:T(8,128)S(1)}, f32[16,16,2048]{2,0,1:T(8,128)S(1)}) fusion(f32[16,3,16,2048]{3,0,2,1:T(8,128)} %copy-done.1, f32[16,2048]{1,0:T(8,128)S(1)} %bitcast.118, f32[16,2048]{1,0:T(8,128)S(1)} %get-tuple-element.8, ...), kind=kLoop, calls=%fused_computation.74 | loop fusion | flops 11534336 | bytes 15597568 | tf_op jit(solution)/shard_map/add | solution.py:98
  140.7 11.7 %fusion.6 = f32[16,3,16,2048]{3,0,2,1:T(8,128)S(1)} fusion(f32[16,3,16,2048]{3,0,2,1:T(8,128)S(1)} %bitcast.113, f32[16,3,1,2048]{3,0,2,1:T(8,128)} %collective-permute-done.1, f32[16,3,1,2048]{3,0,2,1:T(8,128)} %collective-permute-done, f32[16,1,16,2048]{3,0,2,1:T(8,128)S(1)} %get-tuple-element.21, f32[16,1,16,2048]{3,0,2,1:T(8,128)S(1)} %get-tuple-element.20, ...), kind=kLoop, calls=%fused_computation.15 | loop fusion | flops 56623104 | bytes 34996424 | tf_op jit(solution)/shard_map/add | solution.py:107
  152.6 2.6 collective-permute-start.21
  155.3 8.1 %collective-permute-done.20 = f32[16,3,1,2048]{3,0,2,1:T(8,128)S(1)} collective-permute-done((f32[16,3,1,2048]{3,0,2,1:T(8,128)S(1)}, f32[16,3,1,2048]{3,0,2,1:T(8,128)S(1)}, u32[]{:S(2)}, u32[]{:S(2)}) %collective-permute-start.20) | collective-permute-done | bytes 393248 | tf_op jit(solution)/shard_map/ppermute | solution.py:26
  164.6 2.7 multiply_reduce_fusion
  167.4 11.2 %fusion.155 = (f32[16,3,16,2047]{3,0,2,1:T(8,128)}, f32[16,3,16,2047]{3,0,2,1:T(8,128)}) fusion(f32[16,3,16,2048]{3,0,2,1:T(8,128)} %copy-done), kind=kLoop, calls=%fused_computation.299 | loop fusion | bytes 25153536 | tf_op jit(solution)/shard_map/jit(_roll_static)/slice | solution.py:85
  180.7 23.7 %all-reduce.5.cloned.1.call-done = f32[3,18,2048]{2,1,0:T(8,128)} async-done(((f32[3,18,2048]{2,1,0:T(8,128)}), f32[3,18,2048]{2,1,0:T(8,128)}) %all-reduce.5.cloned.1.call-update) | async-done | bytes 442384 | tf_op jit(solution)/shard_map/psum | solution.py:122
  209.4 2.6 collective-permute-done.23
  213.8 2.7 collective-permute-done.25
  218.3 2.7 collective-permute-done.27
  222.8 2.7 collective-permute-done.29
  227.3 2.7 collective-permute-done.31
  231.8 2.7 collective-permute-done.33
  236.3 2.9 %collective-permute-done.35 = f32[2,1,2048]{2,1,0:T(1,128)S(1)} collective-permute-done((f32[2,1,2048]{2,1,0:T(1,128)S(1)}, f32[2,1,2048]{2,1,0:T(1,128)S(1)}, u32[]{:S(2)}, u32[]{:S(2)}) %collective-permute-start.35) | collective-permute-done | bytes 16416 | tf_op jit(solution)/shard_map/ppermute | solution.py:26
  241.5 14.6 %pmax.15 = f32[]{:T(128)} all-reduce(f32[]{:T(128)} %get-tuple-element.48), channel_id=1, replica_groups=mesh['rows'=8,'fields'=4] {'rows'}, use_global_device_ids=true, to_apply=%region_7.8 | all-reduce | flops 1 | bytes 8 | tf_op jit(solution)/shard_map/pmax | solution.py:130
  257.6 3.9 %multiply_add_fusion.2 = (f32[16,1,16,2048]{3,0,2,1:T(8,128)S(1)}, f32[16,1,16,2048]{3,0,2,1:T(8,128)S(1)}, f32[16,1,16,2048]{3,0,2,1:T(8,128)S(1)}, f32[16,16,2048]{2,0,1:T(8,128)S(1)}) fusion(f32[16,3,16,2048]{3,0,2,1:T(8,128)} %copy-done, f32[16,2048]{1,0:T(8,128)S(1)} %get-tuple-element.40, f32[16,2048]{1,0:T(8,128)S(1)} %get-tuple-element.4, ...), kind=kLoop, calls=%fused_computation.70 | loop fusion | flops 11534336 | bytes 15597568 | tf_op jit(solution)/shard_map/add | solution.py:98
  263.8 11.5 %fusion.13 = f32[16,3,16,2048]{3,0,2,1:T(8,128)S(1)} fusion(f32[16,3,16,2048]{3,0,2,1:T(8,128)S(1)} %bitcast.111, f32[16,3,1,2048]{3,0,2,1:T(8,128)S(1)} %collective-permute-done.21, f32[16,3,1,2048]{3,0,2,1:T(8,128)S(1)} %collective-permute-done.20, f32[16,1,16,2048]{3,0,2,1:T(8,128)S(1)} %get-tuple-element.18, ...), kind=kLoop, calls=%fused_computation.22 | loop fusion | flops 56623104 | bytes 34996424 | tf_op jit(solution)/shard_map/add | solution.py:107
  275.3 6.3 %copy.60 = f32[16,3,16,2048]{3,2,1,0:T(8,128)} copy(f32[16,3,16,2048]{3,0,2,1:T(8,128)S(1)} %fusion.13) | data formatting | bytes 12582912
  (216 shorter events, 53.6 us)
Async XLA Ops:
  7.2 73.3 %all-reduce.3.cloned.1.call-start = ((), (), s32[]{:S(2)}) async-start(), calls=%async_computation | async-start | bytes 1179648 | tf_op jit(solution)/shard_map/psum | solution.py:122
  14.7 13.2 %collective-permute-start = (f32[16,3,1,2048]{3,0,2,1:T(8,128)}, f32[16,3,1,2048]{3,0,2,1:T(8,128)}, u32[]{:S(2)}, u32[]{:S(2)}) collective-permute-start(f32[16,3,1,2048]{3,0,2,1:T(8,128)} %get-tuple-element.34), channel_id=1, source_target_pairs={{0,4},{4,8},{8,12},{12,16},{16,20},{20,24},{24,28},{28,0},{1,5},{5... | collective-permute-start | bytes 1179656 | tf_op jit(solution)/shard_map/ppermute | solution.py:26
  15.2 20.2 %collective-permute-start.1 = (f32[16,3,1,2048]{3,0,2,1:T(8,128)}, f32[16,3,1,2048]{3,0,2,1:T(8,128)}, u32[]{:S(2)}, u32[]{:S(2)}) collective-permute-start(f32[16,3,1,2048]{3,0,2,1:T(8,128)} %get-tuple-element.35), channel_id=1, source_target_pairs={{4,0},{8,4},{12,8},{16,12},{20,16},{24,20},{28,24},{0,28},{5,1},{9... | collective-permute-start | bytes 1179656 | tf_op jit(solution)/shard_map/ppermute | solution.py:28
  18.7 63.5 %collective-permute-start.2 = (f32[2,1,2048]{2,1,0:T(1,128)}, f32[2,1,2048]{2,1,0:T(1,128)}, u32[]{:S(2)}, u32[]{:S(2)}) collective-permute-start(f32[2,1,2048]{2,1,0:T(1,128)} %get-tuple-element.155), channel_id=1, source_target_pairs={{4,0},{8,4},{12,8},{16,12},{20,16},{24,20},{28,24},{0,28},{5,1},{9... | collective-permute-start | bytes 49160 | tf_op jit(solution)/shard_map/ppermute | solution.py:28
  19.9 62.3 %collective-permute-start.3 = (f32[2,1,2048]{2,1,0:T(1,128)}, f32[2,1,2048]{2,1,0:T(1,128)}, u32[]{:S(2)}, u32[]{:S(2)}) collective-permute-start(f32[2,1,2048]{2,1,0:T(1,128)} %get-tuple-element.156), channel_id=1, source_target_pairs={{0,4},{4,8},{8,12},{12,16},{16,20},{20,24},{24,28},{28,0},{1,5},{5... | collective-permute-start | bytes 49160 | tf_op jit(solution)/shard_map/ppermute | solution.py:26
  39.7 164.7 %all-reduce.5.cloned.1.call-start = ((), (), s32[]{:S(2)}) async-start(), calls=%async_computation.1 | async-start | bytes 1179648 | tf_op jit(solution)/shard_map/psum | solution.py:122
  83.3 2.9 collective-permute-start.4
  84.7 4.1 %collective-permute-start.5 = (f32[2,1,2048]{2,1,0:T(1,128)S(1)}, f32[2,1,2048]{2,1,0:T(1,128)S(1)}, u32[]{:S(2)}, u32[]{:S(2)}) collective-permute-start(f32[2,1,2048]{2,1,0:T(1,128)S(1)} %get-tuple-element.150), channel_id=1, source_target_pairs={{0,4},{4,8},{8,12},{12,16},{16,20},{20,24},{24,28},{28,0},{1,5},{5... | collective-permute-start | bytes 49160 | tf_op jit(solution)/shard_map/ppermute | solution.py:26
  89.2 4.1 %collective-permute-start.7 = (f32[2,1,2048]{2,1,0:T(1,128)S(1)}, f32[2,1,2048]{2,1,0:T(1,128)S(1)}, u32[]{:S(2)}, u32[]{:S(2)}) collective-permute-start(f32[2,1,2048]{2,1,0:T(1,128)S(1)} %get-tuple-element.144), channel_id=1, source_target_pairs={{0,4},{4,8},{8,12},{12,16},{16,20},{20,24},{24,28},{28,0},{1,5},{5... | collective-permute-start | bytes 49160 | tf_op jit(solution)/shard_map/ppermute | solution.py:26
  93.6 1.5 collective-permute-start.8
  93.7 4.1 %collective-permute-start.9 = (f32[2,1,2048]{2,1,0:T(1,128)S(1)}, f32[2,1,2048]{2,1,0:T(1,128)S(1)}, u32[]{:S(2)}, u32[]{:S(2)}) collective-permute-start(f32[2,1,2048]{2,1,0:T(1,128)S(1)} %get-tuple-element.138), channel_id=1, source_target_pairs={{0,4},{4,8},{8,12},{12,16},{16,20},{20,24},{24,28},{28,0},{1,5},{5... | collective-permute-start | bytes 49160 | tf_op jit(solution)/shard_map/ppermute | solution.py:26
  98.1 4.1 %collective-permute-start.11 = (f32[2,1,2048]{2,1,0:T(1,128)S(1)}, f32[2,1,2048]{2,1,0:T(1,128)S(1)}, u32[]{:S(2)}, u32[]{:S(2)}) collective-permute-start(f32[2,1,2048]{2,1,0:T(1,128)S(1)} %get-tuple-element.132), channel_id=1, source_target_pairs={{0,4},{4,8},{8,12},{12,16},{16,20},{20,24},{24,28},{28,0},{1,5},{5... | collective-permute-start | bytes 49160 | tf_op jit(solution)/shard_map/ppermute | solution.py:26
  102.6 4.1 %collective-permute-start.13 = (f32[2,1,2048]{2,1,0:T(1,128)S(1)}, f32[2,1,2048]{2,1,0:T(1,128)S(1)}, u32[]{:S(2)}, u32[]{:S(2)}) collective-permute-start(f32[2,1,2048]{2,1,0:T(1,128)S(1)} %get-tuple-element.126), channel_id=1, source_target_pairs={{0,4},{4,8},{8,12},{12,16},{16,20},{20,24},{24,28},{28,0},{1,5},{5... | collective-permute-start | bytes 49160 | tf_op jit(solution)/shard_map/ppermute | solution.py:26
  107.1 1.5 collective-permute-start.14
  107.1 4.3 %collective-permute-start.15 = (f32[2,1,2048]{2,1,0:T(1,128)S(1)}, f32[2,1,2048]{2,1,0:T(1,128)S(1)}, u32[]{:S(2)}, u32[]{:S(2)}) collective-permute-start(f32[2,1,2048]{2,1,0:T(1,128)S(1)} %get-tuple-element.120), channel_id=1, source_target_pairs={{0,4},{4,8},{8,12},{12,16},{16,20},{20,24},{24,28},{28,0},{1,5},{5... | collective-permute-start | bytes 49160 | tf_op jit(solution)/shard_map/ppermute | solution.py:26
  111.9 4.1 %collective-permute-start.17 = (f32[2,1,2048]{2,1,0:T(1,128)S(1)}, f32[2,1,2048]{2,1,0:T(1,128)S(1)}, u32[]{:S(2)}, u32[]{:S(2)}) collective-permute-start(f32[2,1,2048]{2,1,0:T(1,128)S(1)} %get-tuple-element.114), channel_id=1, source_target_pairs={{0,4},{4,8},{8,12},{12,16},{16,20},{20,24},{24,28},{28,0},{1,5},{5... | collective-permute-start | bytes 49160 | tf_op jit(solution)/shard_map/ppermute | solution.py:26
  117.8 16.1 %collective-permute-start.18 = (f32[2,1,2048]{2,1,0:T(1,128)S(1)}, f32[2,1,2048]{2,1,0:T(1,128)S(1)}, u32[]{:S(2)}, u32[]{:S(2)}) collective-permute-start(f32[2,1,2048]{2,1,0:T(1,128)S(1)} %get-tuple-element.107), channel_id=1, source_target_pairs={{4,0},{8,4},{12,8},{16,12},{20,16},{24,20},{28,24},{0,28},{5,1},{9... | collective-permute-start | bytes 49160 | tf_op jit(solution)/shard_map/ppermute | solution.py:28
  117.8 16.1 %collective-permute-start.19 = (f32[2,1,2048]{2,1,0:T(1,128)S(1)}, f32[2,1,2048]{2,1,0:T(1,128)S(1)}, u32[]{:S(2)}, u32[]{:S(2)}) collective-permute-start(f32[2,1,2048]{2,1,0:T(1,128)S(1)} %get-tuple-element.108), channel_id=1, source_target_pairs={{0,4},{4,8},{8,12},{12,16},{16,20},{20,24},{24,28},{28,0},{1,5},{5... | collective-permute-start | bytes 49160 | tf_op jit(solution)/shard_map/ppermute | solution.py:26
  152.5 10.9 %collective-permute-start.20 = (f32[16,3,1,2048]{3,0,2,1:T(8,128)S(1)}, f32[16,3,1,2048]{3,0,2,1:T(8,128)S(1)}, u32[]{:S(2)}, u32[]{:S(2)}) collective-permute-start(f32[16,3,1,2048]{3,0,2,1:T(8,128)S(1)} %get-tuple-element.27), channel_id=1, source_target_pairs={{0,4},{4,8},{8,12},{12,16},{16,20},{20,24},{24,28},{28,0},{1,5},{5... | collective-permute-start | bytes 1179656 | tf_op jit(solution)/shard_map/ppermute | solution.py:26
  152.6 10.9 %collective-permute-start.21 = (f32[16,3,1,2048]{3,0,2,1:T(8,128)S(1)}, f32[16,3,1,2048]{3,0,2,1:T(8,128)S(1)}, u32[]{:S(2)}, u32[]{:S(2)}) collective-permute-start(f32[16,3,1,2048]{3,0,2,1:T(8,128)S(1)} %get-tuple-element.28), channel_id=1, source_target_pairs={{4,0},{8,4},{12,8},{16,12},{20,16},{24,20},{28,24},{0,28},{5,1},{9... | collective-permute-start | bytes 1179656 | tf_op jit(solution)/shard_map/ppermute | solution.py:28
  206.5 2.9 collective-permute-start.22
  207.9 4.1 %collective-permute-start.23 = (f32[2,1,2048]{2,1,0:T(1,128)S(1)}, f32[2,1,2048]{2,1,0:T(1,128)S(1)}, u32[]{:S(2)}, u32[]{:S(2)}) collective-permute-start(f32[2,1,2048]{2,1,0:T(1,128)S(1)} %get-tuple-element.96), channel_id=1, source_target_pairs={{0,4},{4,8},{8,12},{12,16},{16,20},{20,24},{24,28},{28,0},{1,5},{5... | collective-permute-start | bytes 49160 | tf_op jit(solution)/shard_map/ppermute | solution.py:26
  212.3 1.5 collective-permute-start.24
  212.4 4.1 %collective-permute-start.25 = (f32[2,1,2048]{2,1,0:T(1,128)S(1)}, f32[2,1,2048]{2,1,0:T(1,128)S(1)}, u32[]{:S(2)}, u32[]{:S(2)}) collective-permute-start(f32[2,1,2048]{2,1,0:T(1,128)S(1)} %get-tuple-element.90), channel_id=1, source_target_pairs={{0,4},{4,8},{8,12},{12,16},{16,20},{20,24},{24,28},{28,0},{1,5},{5... | collective-permute-start | bytes 49160 | tf_op jit(solution)/shard_map/ppermute | solution.py:26
  216.9 4.1 %collective-permute-start.27 = (f32[2,1,2048]{2,1,0:T(1,128)S(1)}, f32[2,1,2048]{2,1,0:T(1,128)S(1)}, u32[]{:S(2)}, u32[]{:S(2)}) collective-permute-start(f32[2,1,2048]{2,1,0:T(1,128)S(1)} %get-tuple-element.84), channel_id=1, source_target_pairs={{0,4},{4,8},{8,12},{12,16},{16,20},{20,24},{24,28},{28,0},{1,5},{5... | collective-permute-start | bytes 49160 | tf_op jit(solution)/shard_map/ppermute | solution.py:26
  221.3 1.5 collective-permute-start.28
  221.4 4.1 %collective-permute-start.29 = (f32[2,1,2048]{2,1,0:T(1,128)S(1)}, f32[2,1,2048]{2,1,0:T(1,128)S(1)}, u32[]{:S(2)}, u32[]{:S(2)}) collective-permute-start(f32[2,1,2048]{2,1,0:T(1,128)S(1)} %get-tuple-element.78), channel_id=1, source_target_pairs={{0,4},{4,8},{8,12},{12,16},{16,20},{20,24},{24,28},{28,0},{1,5},{5... | collective-permute-start | bytes 49160 | tf_op jit(solution)/shard_map/ppermute | solution.py:26
  225.9 4.1 %collective-permute-start.31 = (f32[2,1,2048]{2,1,0:T(1,128)S(1)}, f32[2,1,2048]{2,1,0:T(1,128)S(1)}, u32[]{:S(2)}, u32[]{:S(2)}) collective-permute-start(f32[2,1,2048]{2,1,0:T(1,128)S(1)} %get-tuple-element.72), channel_id=1, source_target_pairs={{0,4},{4,8},{8,12},{12,16},{16,20},{20,24},{24,28},{28,0},{1,5},{5... | collective-permute-start | bytes 49160 | tf_op jit(solution)/shard_map/ppermute | solution.py:26
  230.4 4.1 %collective-permute-start.33 = (f32[2,1,2048]{2,1,0:T(1,128)S(1)}, f32[2,1,2048]{2,1,0:T(1,128)S(1)}, u32[]{:S(2)}, u32[]{:S(2)}) collective-permute-start(f32[2,1,2048]{2,1,0:T(1,128)S(1)} %get-tuple-element.66), channel_id=1, source_target_pairs={{0,4},{4,8},{8,12},{12,16},{16,20},{20,24},{24,28},{28,0},{1,5},{5... | collective-permute-start | bytes 49160 | tf_op jit(solution)/shard_map/ppermute | solution.py:26
  234.9 4.4 %collective-permute-start.35 = (f32[2,1,2048]{2,1,0:T(1,128)S(1)}, f32[2,1,2048]{2,1,0:T(1,128)S(1)}, u32[]{:S(2)}, u32[]{:S(2)}) collective-permute-start(f32[2,1,2048]{2,1,0:T(1,128)S(1)} %get-tuple-element.60), channel_id=1, source_target_pairs={{0,4},{4,8},{8,12},{12,16},{16,20},{20,24},{24,28},{28,0},{1,5},{5... | collective-permute-start | bytes 49160 | tf_op jit(solution)/shard_map/ppermute | solution.py:26
  239.5 17.4 %collective-permute-start.36 = (f32[2,1,2048]{2,1,0:T(1,128)S(1)}, f32[2,1,2048]{2,1,0:T(1,128)S(1)}, u32[]{:S(2)}, u32[]{:S(2)}) collective-permute-start(f32[2,1,2048]{2,1,0:T(1,128)S(1)} %get-tuple-element.53), channel_id=1, source_target_pairs={{4,0},{8,4},{12,8},{16,12},{20,16},{24,20},{28,24},{0,28},{5,1},{9... | collective-permute-start | bytes 49160 | tf_op jit(solution)/shard_map/ppermute | solution.py:28
  239.5 17.3 %collective-permute-start.37 = (f32[2,1,2048]{2,1,0:T(1,128)S(1)}, f32[2,1,2048]{2,1,0:T(1,128)S(1)}, u32[]{:S(2)}, u32[]{:S(2)}) collective-permute-start(f32[2,1,2048]{2,1,0:T(1,128)S(1)} %get-tuple-element.54), channel_id=1, source_target_pairs={{0,4},{4,8},{8,12},{12,16},{16,20},{20,24},{24,28},{28,0},{1,5},{5... | collective-permute-start | bytes 49160 | tf_op jit(solution)/shard_map/ppermute | solution.py:26
  (26 other events, 223.1 us)
Sparse Core Ops, SparseCore 0:
  39.8 40.5 all-reduce.2
  167.5 36.8 all-reduce.4
where the time goes:
time: 289 us; the launch traced here: 288 us
  waiting for transfers between devices  124 us (43%)
  local copies, waits for them, and re-layouts  53.6 us (19%)
  other arithmetic  47.8 us (17%)
  blocking collectives  29.2 us (10%)
  starting transfers between devices  17.9 us (6%)
  between operations  16.4 us (6%)
    psum x2, waiting for transfers between devices, body(): stress = G_COEF / FIELDS * lax.psum(local_total, 'fields')  64.4 us
    ppermute x19, waiting for transfers between devices, with_halo(): lax.ppermute(tail, axis, [(i, (i + 1) % count) for i in range(count)])  46 us
    pmax x2, blocking collectives, body(): lax.pmax(jnp.max(jnp.abs(speed_now[0]) + jnp.abs(speed_now[1])), 'rows')  29.2 us
    unnamed x40, local copies, waits for them, and re-layouts  25 us
    add x2, other arithmetic, advance(): inner + dt * (stretch - advect - spring[:, None] * inner / LAMBDA)  23.2 us
    slice x4, local copies, waits for them, and re-layouts, advance(): east = jnp.roll(inner, -1, axis=-1)  21 us
    ppermute x19, waiting for transfers between devices, with_halo(): lax.ppermute(head, axis, [((i + 1) % count, i) for i in range(count)])  13.1 us
    ppermute x19, starting transfers between devices, with_halo(): lax.ppermute(head, axis, [((i + 1) % count, i) for i in range(count)])  10.4 us
  transfers between devices with their start and end apart: 40, of which 31 were waited for; matrix products, arithmetic and copies ran while one was open for 13% of the time, Pallas kernels for 0%

commit v1 on v0

v1 whole, which is shorter than its diff:
```python
import functools

import jax
import jax.numpy as jnp
from jax import lax
from jax.experimental import pallas as pl
from jax.experimental.pallas import tpu as pltpu
from jax.sharding import PartitionSpec as P

FIELDS = 64
SWEEPS = 8
STEPS = 2

G_COEF = 4.0
ALPHA = 0.05
LMAX2 = 20.0
LAMBDA = 1.0
DT = 0.2
SIGMA = 1.0

K = 8
LAG = 2
MESH = pl.DeviceIdType.MESH


def widened(load, start, width, total):
    lo, hi = start - 128, start + width + 128
    if lo < 0:
        return jnp.concatenate([load(total + lo, total), load(0, hi)], axis=1)
    if hi > total:
        return jnp.concatenate([load(lo, total), load(0, hi - total)], axis=1)
    return load(lo, hi)


def west_east(load, start, width, total):
    wide = widened(load, start, width, total)
    span = width + 256
    west = pltpu.roll(wide, 1, 1)[:, 128:-128]
    east = pltpu.roll(wide, span - 1, 1)[:, 128:-128]
    return west, east


def south_north(rows):
    count = rows.shape[0]
    return pltpu.roll(rows, 1, 0), pltpu.roll(rows, count - 1, 0)


def kernel(
    R, F, seeds, dev, vel, frc, out_d, out_u,
    D, NZ, ST, SES, SER, ES, ER, U48, UU, RH, FP, CA, CB, TT, COEF, SPR,
    in_sem, out_sem, ses_s, ses_r, u_s, u_r, es_s, es_r,
    in_s, a_r, b_r, t_s, rh_s, rh_r, sp_s, sp_r,
):
    nf, NY = dev.shape[0], dev.shape[3]
    r = lax.axis_index("rows")
    f = lax.axis_index("fields")
    south = {"rows": lax.rem(r + R - 1, R)}
    north = {"rows": lax.rem(r + 1, R)}
    half = F // 2
    is_low = f < half
    inward = {"fields": jnp.where(is_low, f + 1, f - 1)}
    outward_index = jnp.where(is_low, f - 1, f + 1)
    not_end = jnp.logical_and(f > 0, f < F - 1)
    is_mid = jnp.logical_or(f == half - 1, f == half)
    outward = {"fields": jnp.clip(outward_index, 0, F - 1)}
    CW = NY // K
    W = 512
    NC = NY // W

    def remote(src, dst, s, q, device):
        return pltpu.make_async_remote_copy(
            src_ref=src, dst_ref=dst, send_sem=s, recv_sem=q, device_id=device, device_id_type=MESH
        )

    loads = [
        pltpu.make_async_copy(
            dev.at[:, :, :, pl.ds(c * W, W)], D.at[0, :, :, :, pl.ds(c * W, W)], in_sem.at[c]
        )
        for c in range(NC)
    ]
    for one in loads:
        one.start()

    barrier = pltpu.get_barrier_semaphore()
    for p in range(1, R):
        pl.semaphore_signal(barrier, inc=1, device_id={"rows": lax.rem(r + p, R)}, device_id_type=MESH)
    pl.semaphore_signal(barrier, inc=1, device_id=inward, device_id_type=MESH)

    @pl.when(not_end)
    def _():
        pl.semaphore_signal(barrier, inc=1, device_id=outward, device_id_type=MESH)

    def ses_copy(step, side):
        return remote(SES.at[step, side], SER.at[step, 1 - side], ses_s.at[step, side],
                      ses_r.at[step, 1 - side], south if side == 0 else north)

    def es_copy(step, side):
        return remote(ES.at[step, side], ER.at[step, 1 - side], es_s.at[step, side],
                      es_r.at[step, 1 - side], south if side == 0 else north)

    def u_copy(step, side):
        src = U48.at[step, :, pl.ds(16, 16)]
        dst = U48.at[step, :, pl.ds(32 if side == 0 else 0, 16)]
        return remote(src, dst, u_s.at[step, side], u_r.at[step, 1 - side], south if side == 0 else north)

    def cols(c):
        return pl.ds(c * CW, CW)

    def in_copy(step, c):
        return remote(FP.at[step, :, :, cols(c)], CA.at[step, :, :, cols(c)], in_s.at[step, c],
                      a_r.at[step, c], inward)

    def mid_copy(step, c):
        return remote(FP.at[step, :, :, cols(c)], CB.at[step, :, :, cols(c)], in_s.at[step, c],
                      b_r.at[step, c], inward)

    def total_copy(step, c):
        return remote(TT.at[step, :, :, cols(c)], CB.at[step, :, :, cols(c)], t_s.at[step, c],
                      b_r.at[step, c], outward)

    def rh_copy(step, side, c):
        src = RH.at[step, :, pl.ds(8 if side == 0 else 16, 8), cols(c)]
        dst = RH.at[step, :, pl.ds(24 if side == 0 else 0, 8), cols(c)]
        return remote(src, dst, rh_s.at[step, side, c], rh_r.at[step, 1 - side, c],
                      south if side == 0 else north)

    def sp_copy(step, p):
        return remote(SPR.at[step, 0], SPR.at[step, p], sp_s.at[step, p], sp_r.at[step, p],
                      {"rows": lax.rem(r + p, R)})

    def stress(step):
        for c in range(NC):
            if step == 0:
                loads[c].wait()
            at = slice(c * W, c * W + W)

            def add(i, acc):
                tensor = [D[step, i, m, :, at] for m in range(3)]
                for m in range(3):
                    ES[step, 0, pl.ds(3 * i + m, 1), at] = tensor[m][0:1]
                    ES[step, 1, pl.ds(3 * i + m, 1), at] = tensor[m][15:16]
                spring = (1.0 + 2.0 / LMAX2) + (tensor[0] + tensor[2]) * (1.0 / LMAX2)
                return tuple(acc[m] + spring * tensor[m] for m in range(3))

            zero = jnp.zeros((16, W), jnp.float32)
            acc = lax.fori_loop(0, nf, add, (zero, zero, zero))
            acc = [one * (G_COEF / FIELDS) for one in acc]
            for m in range(3):
                ST[m, :, at] = acc[m]
            for m in (1, 2):
                row = (m - 1) * NC + c
                SES[step, 0, row:row + 1, :] = acc[m][0:1]
                SES[step, 1, row:row + 1, :] = acc[m][15:16]

    row16 = lax.broadcasted_iota(jnp.int32, (16, W), 0)

    def with_edges(rows, low, high):
        down, up = south_north(rows)
        return jnp.where(row16 == 0, low, down), jnp.where(row16 == 15, high, up)

    def force(step, c):
        at = slice(c * W, c * W + W)
        for comp in range(2):
            west, east = west_east(lambda lo, hi: ST[comp, :, lo:hi], c * W, W, NY)
            row = comp * NC + c
            down, up = with_edges(ST[comp + 1, :, at], SER[step, 0, row:row + 1, :], SER[step, 1, row:row + 1, :])
            FP[step, comp, :, at] = ((east - west) + (up - down)) * 0.5

    iota_cells = lax.broadcasted_iota(jnp.int32, (16, W), 0) * NY + lax.broadcasted_iota(jnp.int32, (16, W), 1)

    def noise(step, lo, hi):
        if hi <= lo:
            return

        def one(i, _):
            base = seeds[i] * jnp.int32(2654435) + r * jnp.int32(16 * NY)
            for c in range(NC):
                for m in range(3):
                    h = iota_cells + (base + jnp.int32((3 * step + m) * 97531 + c * W))
                    h = jnp.bitwise_xor(h, lax.shift_right_logical(h, jnp.full_like(h, 16)))
                    h = h * jnp.int32(73244475)
                    h = jnp.bitwise_xor(h, lax.shift_right_logical(h, jnp.full_like(h, 16)))
                    h = h * jnp.int32(73244475)
                    h = jnp.bitwise_xor(h, lax.shift_right_logical(h, jnp.full_like(h, 16)))
                    h = jnp.bitwise_and(h, jnp.int32(65535)).astype(jnp.float32)
                    NZ[i, m, :, c * W:c * W + W] = (h - 32767.5) * (SIGMA / 18918.6)
            return 0

        lax.fori_loop(lo, hi, one, 0)

    def chain(step):
        for i in range(K + LAG):
            if i < K:
                @pl.when(not_end)
                def _():
                    in_copy(step, i).wait_recv()
                    at = slice(i * CW, i * CW + CW)
                    FP[step, :, :, at] = FP[step, :, :, at] + CA[step, :, :, at]

                @pl.when(is_mid)
                def _():
                    mid_copy(step, i).start()

                @pl.when(jnp.logical_not(is_mid))
                def _():
                    in_copy(step, i).start()

                noise(step, i * nf // 16, (i + 1) * nf // 16)
            if i >= LAG:
                j = i - LAG
                at = slice(j * CW, j * CW + CW)
                mid_copy(step, j).wait_recv()
                got = CB[step, :, :, at]
                total = jnp.where(is_mid, FP[step, :, :, at] + got, got)
                TT[step, :, :, at] = total

                @pl.when(not_end)
                def _():
                    total_copy(step, j).start()

                RH[step, :, 8:24, at] = frc[:, :, at] + total
                rh_copy(step, 0, j).start()
                rh_copy(step, 1, j).start()

    factor = 1.0 / (ALPHA + 4.0)

    def solve(step):
        for comp in range(2):
            for c in range(NC):
                at = slice(c * W, c * W + W)
                west, east = west_east(lambda lo, hi: U48[step, comp, 8:40, lo:hi], c * W, W, NY)
                down, up = south_north(U48[step, comp, :, at])
                beside = (up[8:40] + down[8:40]) + (east + west)
                UU[1, comp, :, at] = (RH[step, comp, :, at] + beside) * factor

        def sweep(k, _):
            src, dst = lax.rem(k + 1, 2), lax.rem(k, 2)
            for comp in range(2):
                for c in range(NC):
                    at = slice(c * W, c * W + W)
                    west, east = west_east(lambda lo, hi: UU[src, comp, :, lo:hi], c * W, W, NY)
                    down, up = south_north(UU[src, comp, :, at])
                    UU[dst, comp, :, at] = (RH[step, comp, :, at] + ((up + down) + (east + west))) * factor
            return 0

        lax.fori_loop(2, SWEEPS + 1, sweep, 0)

    def local_speed(step):
        top = None
        for c in range(NC):
            at = slice(c * W, c * W + W)
            one = jnp.abs(UU[0, 0, 8:24, at]) + jnp.abs(UU[0, 1, 8:24, at])
            one = jnp.maximum(one[0:8], one[8:16])
            for q in range(W // 128):
                part = one[:, q * 128:q * 128 + 128]
                top = part if top is None else jnp.maximum(top, part)
        SPR[step, 0] = top
        for p in range(1, R):
            sp_copy(step, p).start()

    def coefficients(step):
        top = SPR[step, 0]
        for p in range(1, R):
            sp_copy(step, p).wait_recv()
            top = jnp.maximum(top, SPR[step, p])
        top = jnp.max(jnp.max(top, axis=1, keepdims=True), axis=0, keepdims=True)
        dt = DT / (1.0 + top)
        root = jnp.sqrt(dt)
        for c in range(NC):
            at = slice(c * W, c * W + W)
            grads = []
            for comp in range(2):
                west, east = west_east(lambda lo, hi: UU[0, comp, 8:24, lo:hi], c * W, W, NY)
                down, up = south_north(UU[0, comp, :, at])
                grads.append((east - west) * 0.5)
                grads.append((up[8:24] - down[8:24]) * 0.5)
            lxx, lxy, lyx, lyy = [one * dt for one in grads]
            ux, uy = UU[0, 0, 8:24, at] * dt, UU[0, 1, 8:24, at] * dt
            centre = 1.0 - (jnp.abs(ux) + jnp.abs(uy)) - dt * ((1.0 + 2.0 / LMAX2) / LAMBDA)
            values = (
                jnp.maximum(ux, 0.0), -jnp.minimum(ux, 0.0), jnp.maximum(uy, 0.0), -jnp.minimum(uy, 0.0),
                centre + 2.0 * lxx, centre + (lxx + lyy), centre + 2.0 * lyy,
                lxy, lyx, lxx + lxx, lxy + lyx, lyy + lyy,
            )
            for k, one in enumerate(values):
                COEF[k, :, at] = one
        return dt, root

    AW = 256
    row_a = lax.broadcasted_iota(jnp.int32, (16, AW), 0)

    def store_out(i):
        return pltpu.make_async_copy(D.at[0, i], out_d.at[i], out_sem.at[i])

    def advance(step, dt, root):
        pull = jnp.broadcast_to(dt * (1.0 / (LMAX2 * LAMBDA)), (16, AW))
        loud = jnp.broadcast_to(root, (16, AW))

        def one(i, _):
            for c in range(NY // AW):
                at = slice(c * AW, c * AW + AW)
                a, b, d = [D[step, i, m, :, at] for m in range(3)]
                q = (a + d) * pull
                lxy, lyx = COEF[7, :, at], COEF[8, :, at]
                xb, yb = lxy * b, lyx * b
                cross = (xb + xb, lxy * d + lyx * a, yb + yb)
                for m, x in enumerate((a, b, d)):
                    west, east = west_east(lambda lo, hi: D[step, i, m, :, lo:hi], c * AW, AW, NY)
                    down, up = south_north(x)
                    down = jnp.where(row_a == 0, ER[step, 0, pl.ds(3 * i + m, 1), at], down)
                    up = jnp.where(row_a == 15, ER[step, 1, pl.ds(3 * i + m, 1), at], up)
                    fresh = (COEF[4 + m, :, at] - q) * x + cross[m]
                    fresh = fresh + (COEF[0, :, at] * west + COEF[1, :, at] * east)
                    fresh = fresh + (COEF[2, :, at] * down + COEF[3, :, at] * up)
                    D[1 - step, i, m, :, at] = fresh + (COEF[9 + m, :, at] + loud * NZ[i, m, :, at])
            if step == STEPS - 1:
                store_out(i).start()
            return 0

        lax.fori_loop(0, nf, one, 0)

    U48[0, :, 16:32] = vel[...]
    for step in range(STEPS):
        stress(step)
        if step == 0:
            pl.semaphore_wait(barrier, jnp.where(not_end, R + 1, R))
        for side in range(2):
            ses_copy(step, side).start()
        if step == 0:
            for side in range(2):
                u_copy(step, side).start()
        for side in range(2):
            es_copy(step, side).start()
        for side in range(2):
            ses_copy(step, side).wait_recv()
        for c in range(NC):
            force(step, c)
        chain(step)
        noise(step, nf // 2, 3 * nf // 4)
        for side in range(2):
            u_copy(step, side).wait_recv()
            for c in range(K):
                rh_copy(step, side, c).wait_recv()
        solve(step)
        local_speed(step)
        if step < STEPS - 1:
            U48[step + 1, :, 16:32] = UU[0, :, 8:24]
            for side in range(2):
                u_copy(step + 1, side).start()
        else:
            out_u[...] = UU[0, :, 8:24]
        noise(step, 3 * nf // 4, nf)
        dt, root = coefficients(step)
        for side in range(2):
            es_copy(step, side).wait_recv()
        advance(step, dt, root)

    for step in range(STEPS):
        for side in range(2):
            ses_copy(step, side).wait_send()
            u_copy(step, side).wait_send()
            es_copy(step, side).wait_send()
        for c in range(K):
            in_copy(step, c).wait_send()
            rh_copy(step, 0, c).wait_send()
            rh_copy(step, 1, c).wait_send()
        for p in range(1, R):
            sp_copy(step, p).wait_send()

        @pl.when(not_end)
        def _():
            for c in range(K):
                total_copy(step, c).wait_send()

    def finish(i, _):
        store_out(i).wait()
        return 0

    lax.fori_loop(0, nf, finish, 0)


def body(R, F, deviation, seeds, velocity, forcing):
    nf, _, rows, NY = deviation.shape
    f32 = jnp.float32
    S = STEPS
    dma = pltpu.SemaphoreType.DMA
    vmem = lambda *shape: pltpu.VMEM(shape, f32)
    return pl.pallas_call(
        functools.partial(kernel, R, F),
        out_shape=(
            jax.ShapeDtypeStruct(deviation.shape, f32),
            jax.ShapeDtypeStruct(velocity.shape, f32),
        ),
        in_specs=[
            pl.BlockSpec(memory_space=pltpu.SMEM),
            pl.BlockSpec(memory_space=pl.ANY),
            pl.BlockSpec(memory_space=pltpu.VMEM),
            pl.BlockSpec(memory_space=pltpu.VMEM),
        ],
        out_specs=(pl.BlockSpec(memory_space=pl.ANY), pl.BlockSpec(memory_space=pltpu.VMEM)),
        scratch_shapes=[
            vmem(2, nf, 3, rows, NY), vmem(nf, 3, rows, NY), vmem(3, rows, NY),
            vmem(S, 2, 8, 512), vmem(S, 2, 8, 512),
            vmem(S, 2, nf * 3, NY), vmem(S, 2, nf * 3, NY),
            vmem(S, 2, 48, NY), vmem(2, 2, 32, NY), vmem(S, 2, 32, NY),
            vmem(S, 2, rows, NY), vmem(S, 2, rows, NY), vmem(S, 2, rows, NY), vmem(S, 2, rows, NY),
            vmem(12, rows, NY), vmem(S, R, 8, 128),
            dma((4,)), dma((nf,)),
            dma((S, 2)), dma((S, 2)), dma((S, 2)), dma((S, 2)), dma((S, 2)), dma((S, 2)),
            dma((S, K)), dma((S, K)), dma((S, K)), dma((S, K)),
            dma((S, 2, K)), dma((S, 2, K)), dma((S, R)), dma((S, R)),
        ],
        compiler_params=pltpu.CompilerParams(
            collective_id=0, has_side_effects=True, vmem_limit_bytes=52 * 1024 * 1024
        ),
    )(seeds, deviation, velocity, forcing)


def solution(mesh):
    return jax.shard_map(
        functools.partial(body, mesh.shape["rows"], mesh.shape["fields"]),
        mesh=mesh,
        in_specs=(
            P("fields", None, "rows", None),
            P("fields"),
            P(None, "rows", None),
            P(None, "rows", None),
        ),
        out_specs=(P("fields", None, "rows", None), P(None, "rows", None)),
        check_vma=False,
    )
```

time: 289 us -> 145 us (0.50)
  Pallas kernels: 0 us -> 135 us
  waiting for transfers between devices: 124 us -> 0 us
  other arithmetic: 47.8 us -> 0 us
  local copies, waits for them, and re-layouts: 53.6 us -> 9.54 us
  blocking collectives: 29.2 us -> 0 us
  starting transfers between devices: 17.9 us -> 0 us
  between operations: 16.4 us -> 0.65 us
    pallas_call x0 -> x1, Pallas kernels: none -> 135 us  [body(): pl.pallas_call(functools.partial(kernel, R, F), out_shape=(jax.ShapeDtype...]
    psum x2 -> x0, waiting for transfers between devices: 64.4 us -> none  [body(): stress = G_COEF / FIELDS * lax.psum(local_total, 'fields')]
    ppermute x38 -> x0, waiting for transfers between devices: 59.1 us -> none  [the longest x19 46 us: with_halo(): lax.ppermute(tail, axis, [(i, (i + 1) % count) for i in range(count)])]
    add x11 -> x0, other arithmetic: 31.7 us -> none  [the longest x2 23.2 us: advance(): inner + dt * (stretch - advect - spring[:, None] * inner / LAMBDA)]
    pmax x2 -> x0, blocking collectives: 29.2 us -> none  [body(): lax.pmax(jnp.max(jnp.abs(speed_now[0]) + jnp.abs(speed_now[1])), 'rows')]
    slice x59 -> x0, local copies, waits for them, and re-layouts: 26.6 us -> none  [the longest x4 21 us: advance(): east = jnp.roll(inner, -1, axis=-1)]
    ppermute x38 -> x0, starting transfers between devices: 17.8 us -> none  [the longest x19 10.4 us: with_halo(): lax.ppermute(head, axis, [((i + 1) % count, i) for i in range(count)])]
    unnamed x40 -> x8, local copies, waits for them, and re-layouts: 25 us -> 9.54 us
  transfers between devices with their start and end apart: 40 -> 0, of which waited for: 31 -> 0; matrix products, arithmetic and copies ran while one was open for 13% -> 0% of each run, Pallas kernels for 0% -> 0%
where the time goes in v1:
time: 145 us
  Pallas kernels  135 us (93%)
  local copies, waits for them, and re-layouts  9.54 us (7%)
    pallas_call x1, Pallas kernels, body(): pl.pallas_call(functools.partial(kernel, R, F), out_shape=(jax.ShapeDtype...  135 us
    unnamed x8, local copies, waits for them, and re-layouts  9.54 us

profile of v1, /device:TPU:0, one launch (start us, length us, event | category | flops | bytes accessed | tf_op | source)
XLA Modules:
  0.0 145.1 jit_solution(17562733922653460750)
XLA Ops:
  0.6 0.0 copy-start
  0.6 0.9 copy-done
  1.6 0.0 copy-start.1
  1.6 0.9 copy-done.1
  2.5 0.0 copy-start.2
  2.5 0.7 copy-done.2
  3.2 134.9 %shard_map.59 = (f32[16,3,16,2048]{3,2,1,0:T(8,128)}, f32[2,16,2048]{2,1,0:T(8,128)S(1)}) custom-call(s32[16]{0:T(128)S(1)} %copy-done.2, f32[16,3,16,2048]{3,2,1,0:T(8,128)} %dev.1, f32[2,16,2048]{2,1,0:T(8,128)S(1)} %copy-done, f32[2,16,2048]{2,1,0:T(8,128)S(1)} %copy-done.1), custom_call_target="tpu_custom_call" | custom-call | tf_op jit(solution)/shard_map/pallas_call | solution.py:388
  138.1 6.3 %copy.8 = f32[16,3,16,2048]{3,2,1,0:T(8,128)} copy(f32[16,3,16,2048]{3,2,1,0:T(8,128)} %get-tuple-element.4) | data formatting | bytes 12582912
  144.4 0.7 copy.9
Async XLA Ops:
  0.6 1.0 copy-start
  1.6 0.9 copy-start.1
  2.5 0.7 copy-start.2

commit v2 on v1

--- a/solution.py
+++ b/solution.py
@@ -40,15 +40,28 @@
     return west, east
 
 
+def tiles_with_sides(load, count):
+    before = pltpu.roll(load(count - 1), 1, 1)
+    here = load(0)
+    here_w, here_e = pltpu.roll(here, 1, 1), pltpu.roll(here, 127, 1)
+    lane = lax.broadcasted_iota(jnp.int32, here.shape, 1)
+    first, last = lane == 0, lane == 127
+    for j in range(count):
+        after = load((j + 1) % count)
+        after_w, after_e = pltpu.roll(after, 1, 1), pltpu.roll(after, 127, 1)
+        yield j, here, jnp.where(first, before, here_w), jnp.where(last, after_e, here_e)
+        before, here, here_w, here_e = here_w, after, after_w, after_e
+
+
 def south_north(rows):
     count = rows.shape[0]
     return pltpu.roll(rows, 1, 0), pltpu.roll(rows, count - 1, 0)
 
 
 def kernel(
-    R, F, seeds, dev, vel, frc, out_d, out_u,
-    D, NZ, ST, SES, SER, ES, ER, U48, UU, RH, FP, CA, CB, TT, COEF, SPR,
-    in_sem, out_sem, ses_s, ses_r, u_s, u_r, es_s, es_r,
+    R, F, seeds_in, dev, vel, frc, out_d, out_u,
+    D, NZ, ST, SES, SER, ES, ER, U32, XS, XR, UU, RH, FR, SD, FP, CA, CB, TT, COEF, SPR,
+    in_sem, arg_sem, out_sem, ses_s, ses_r, u_s, u_r, x_s, x_r, es_s, es_r,
     in_s, a_r, b_r, t_s, rh_s, rh_r, sp_s, sp_r,
 ):
     nf, NY = dev.shape[0], dev.shape[3]
@@ -81,6 +94,12 @@
     for one in loads:
         one.start()
 
+    seed_load = pltpu.make_async_copy(seeds_in, SD, arg_sem.at[0])
+    vel_load = pltpu.make_async_copy(vel, U32.at[0, :, pl.ds(8, 16)], arg_sem.at[1])
+    frc_load = pltpu.make_async_copy(frc, FR, arg_sem.at[2])
+    vel_load.start()
+    frc_load.start()
+    seed_load.start()
     barrier = pltpu.get_barrier_semaphore()
     for p in range(1, R):
         pl.semaphore_signal(barrier, inc=1, device_id={"rows": lax.rem(r + p, R)}, device_id_type=MESH)
@@ -99,9 +118,24 @@
                       es_r.at[step, 1 - side], south if side == 0 else north)
 
     def u_copy(step, side):
-        src = U48.at[step, :, pl.ds(16, 16)]
-        dst = U48.at[step, :, pl.ds(32 if side == 0 else 0, 16)]
+        src = U32.at[step, :, pl.ds(8 if side == 0 else 16, 8)]
+        dst = U32.at[step, :, pl.ds(24 if side == 0 else 0, 8)]
         return remote(src, dst, u_s.at[step, side], u_r.at[step, 1 - side], south if side == 0 else north)
+
+    def x_copy(step, side):
+        return remote(XS.at[step, side], XR.at[step, 1 - side], x_s.at[step, side],
+                      x_r.at[step, 1 - side], south if side == 0 else north)
+
+    def send_velocity(step):
+        for comp in range(2):
+            for c in range(NC):
+                row = comp * NC + c
+                at = slice(c * W, c * W + W)
+                XS[step, 0, row:row + 1, :] = U32[step, comp, 16:24, at][0:1]
+                XS[step, 1, row:row + 1, :] = U32[step, comp, 8:16, at][7:8]
+        for side in range(2):
+            u_copy(step, side).start()
+            x_copy(step, side).start()
 
     def cols(c):
         return pl.ds(c * CW, CW)
@@ -173,7 +207,7 @@
             return
 
         def one(i, _):
-            base = seeds[i] * jnp.int32(2654435) + r * jnp.int32(16 * NY)
+            base = SD[i] * jnp.int32(2654435) + r * jnp.int32(16 * NY)
             for c in range(NC):
                 for m in range(3):
                     h = iota_cells + (base + jnp.int32((3 * step + m) * 97531 + c * W))
@@ -183,7 +217,7 @@
                     h = h * jnp.int32(73244475)
                     h = jnp.bitwise_xor(h, lax.shift_right_logical(h, jnp.full_like(h, 16)))
                     h = jnp.bitwise_and(h, jnp.int32(65535)).astype(jnp.float32)
-                    NZ[i, m, :, c * W:c * W + W] = (h - 32767.5) * (SIGMA / 18918.6)
+                    NZ[i, m, :, c * W:c * W + W] = h
             return 0
 
         lax.fori_loop(lo, hi, one, 0)
@@ -218,28 +252,35 @@
                 def _():
                     total_copy(step, j).start()
 
-                RH[step, :, 8:24, at] = frc[:, :, at] + total
+                RH[step, :, 8:24, at] = FR[:, :, at] + total
                 rh_copy(step, 0, j).start()
                 rh_copy(step, 1, j).start()
 
     factor = 1.0 / (ALPHA + 4.0)
 
+    NT = NY // 128
+
     def solve(step):
+        row32 = lax.broadcasted_iota(jnp.int32, (32, 128), 0)
         for comp in range(2):
-            for c in range(NC):
-                at = slice(c * W, c * W + W)
-                west, east = west_east(lambda lo, hi: U48[step, comp, 8:40, lo:hi], c * W, W, NY)
-                down, up = south_north(U48[step, comp, :, at])
-                beside = (up[8:40] + down[8:40]) + (east + west)
-                UU[1, comp, :, at] = (RH[step, comp, :, at] + beside) * factor
+            for j, here, west, east in tiles_with_sides(
+                lambda j: U32[step, comp, :, j * 128:j * 128 + 128], NT
+            ):
+                at = slice(j * 128, j * 128 + 128)
+                row, part = comp * NC + j * 128 // W, j * 128 % W
+                down, up = south_north(here)
+                down = jnp.where(row32 == 0, XR[step, 0, row:row + 1, part:part + 128], down)
+                up = jnp.where(row32 == 31, XR[step, 1, row:row + 1, part:part + 128], up)
+                UU[1, comp, :, at] = (RH[step, comp, :, at] + ((up + down) + (east + west))) * factor
 
         def sweep(k, _):
             src, dst = lax.rem(k + 1, 2), lax.rem(k, 2)
             for comp in range(2):
-                for c in range(NC):
-                    at = slice(c * W, c * W + W)
-                    west, east = west_east(lambda lo, hi: UU[src, comp, :, lo:hi], c * W, W, NY)
-                    down, up = south_north(UU[src, comp, :, at])
+                for j, here, west, east in tiles_with_sides(
+                    lambda j: UU[src, comp, :, j * 128:j * 128 + 128], NT
+                ):
+                    at = slice(j * 128, j * 128 + 128)
+                    down, up = south_north(here)
                     UU[dst, comp, :, at] = (RH[step, comp, :, at] + ((up + down) + (east + west))) * factor
             return 0
 
@@ -265,7 +306,8 @@
             top = jnp.maximum(top, SPR[step, p])
         top = jnp.max(jnp.max(top, axis=1, keepdims=True), axis=0, keepdims=True)
         dt = DT / (1.0 + top)
-        root = jnp.sqrt(dt)
+        loud = jnp.sqrt(dt) * (SIGMA / 18918.6)
+        shift = loud * 32767.5
         for c in range(NC):
             at = slice(c * W, c * W + W)
             grads = []
@@ -280,38 +322,46 @@
             values = (
                 jnp.maximum(ux, 0.0), -jnp.minimum(ux, 0.0), jnp.maximum(uy, 0.0), -jnp.minimum(uy, 0.0),
                 centre + 2.0 * lxx, centre + (lxx + lyy), centre + 2.0 * lyy,
-                lxy, lyx, lxx + lxx, lxy + lyx, lyy + lyy,
+                lxy, lyx, (lxx + lxx) - shift, (lxy + lyx) - shift, (lyy + lyy) - shift,
             )
             for k, one in enumerate(values):
                 COEF[k, :, at] = one
-        return dt, root
-
-    AW = 256
-    row_a = lax.broadcasted_iota(jnp.int32, (16, AW), 0)
+        return dt, loud
+
+    row_a = lax.broadcasted_iota(jnp.int32, (16, 128), 0)
 
     def store_out(i):
         return pltpu.make_async_copy(D.at[0, i], out_d.at[i], out_sem.at[i])
 
-    def advance(step, dt, root):
-        pull = jnp.broadcast_to(dt * (1.0 / (LMAX2 * LAMBDA)), (16, AW))
-        loud = jnp.broadcast_to(root, (16, AW))
+    def advance(step, dt, loud):
+        pull = jnp.broadcast_to(dt * (1.0 / (LMAX2 * LAMBDA)), (16, 128))
+        loud = jnp.broadcast_to(loud, (16, 128))
 
         def one(i, _):
-            for c in range(NY // AW):
-                at = slice(c * AW, c * AW + AW)
-                a, b, d = [D[step, i, m, :, at] for m in range(3)]
+            def walk(m):
+                return tiles_with_sides(lambda j: D[step, i, m, :, j * 128:j * 128 + 128], NT)
+
+            for both in zip(walk(0), walk(1), walk(2)):
+                j = both[0][0]
+                at = slice(j * 128, j * 128 + 128)
+                if j % 2 == 0:
+                    pair = slice(j * 128, j * 128 + 256)
+                    rims = [
+                        [ER[step, side, pl.ds(3 * i + m, 1), pair] for m in range(3)] for side in range(2)
+                    ]
+                part = slice(j % 2 * 128, j % 2 * 128 + 128)
+                a, b, d = [one[1] for one in both]
                 q = (a + d) * pull
-                lxy, lyx = COEF[7, :, at], COEF[8, :, at]
-                xb, yb = lxy * b, lyx * b
-                cross = (xb + xb, lxy * d + lyx * a, yb + yb)
-                for m, x in enumerate((a, b, d)):
-                    west, east = west_east(lambda lo, hi: D[step, i, m, :, lo:hi], c * AW, AW, NY)
+                xb, yb = COEF[7, :, at] * b, COEF[8, :, at] * b
+                cross = (xb + xb, COEF[7, :, at] * d + COEF[8, :, at] * a, yb + yb)
+                cw, ce, cs, cn = [COEF[k, :, at] for k in range(4)]
+                for m, (_, x, west, east) in enumerate(both):
                     down, up = south_north(x)
-                    down = jnp.where(row_a == 0, ER[step, 0, pl.ds(3 * i + m, 1), at], down)
-                    up = jnp.where(row_a == 15, ER[step, 1, pl.ds(3 * i + m, 1), at], up)
+                    down = jnp.where(row_a == 0, rims[0][m][:, part], down)
+                    up = jnp.where(row_a == 15, rims[1][m][:, part], up)
                     fresh = (COEF[4 + m, :, at] - q) * x + cross[m]
-                    fresh = fresh + (COEF[0, :, at] * west + COEF[1, :, at] * east)
-                    fresh = fresh + (COEF[2, :, at] * down + COEF[3, :, at] * up)
+                    fresh = fresh + (cw * west + ce * east)
+                    fresh = fresh + (cs * down + cn * up)
                     D[1 - step, i, m, :, at] = fresh + (COEF[9 + m, :, at] + loud * NZ[i, m, :, at])
             if step == STEPS - 1:
                 store_out(i).start()
@@ -319,7 +369,6 @@
 
         lax.fori_loop(0, nf, one, 0)
 
-    U48[0, :, 16:32] = vel[...]
     for step in range(STEPS):
         stress(step)
         if step == 0:
@@ -327,8 +376,10 @@
         for side in range(2):
             ses_copy(step, side).start()
         if step == 0:
-            for side in range(2):
-                u_copy(step, side).start()
+            vel_load.wait()
+            send_velocity(step)
+            frc_load.wait()
+            seed_load.wait()
         for side in range(2):
             es_copy(step, side).start()
         for side in range(2):
@@ -339,26 +390,27 @@
         noise(step, nf // 2, 3 * nf // 4)
         for side in range(2):
             u_copy(step, side).wait_recv()
+            x_copy(step, side).wait_recv()
             for c in range(K):
                 rh_copy(step, side, c).wait_recv()
         solve(step)
         local_speed(step)
         if step < STEPS - 1:
-            U48[step + 1, :, 16:32] = UU[0, :, 8:24]
-            for side in range(2):
-                u_copy(step + 1, side).start()
+            U32[step + 1, :, 8:24] = UU[0, :, 8:24]
+            send_velocity(step + 1)
         else:
             out_u[...] = UU[0, :, 8:24]
         noise(step, 3 * nf // 4, nf)
-        dt, root = coefficients(step)
+        dt, loud = coefficients(step)
         for side in range(2):
             es_copy(step, side).wait_recv()
-        advance(step, dt, root)
+        advance(step, dt, loud)
 
     for step in range(STEPS):
         for side in range(2):
             ses_copy(step, side).wait_send()
             u_copy(step, side).wait_send()
+            x_copy(step, side).wait_send()
             es_copy(step, side).wait_send()
         for c in range(K):
             in_copy(step, c).wait_send()
@@ -392,26 +444,27 @@
             jax.ShapeDtypeStruct(velocity.shape, f32),
         ),
         in_specs=[
-            pl.BlockSpec(memory_space=pltpu.SMEM),
             pl.BlockSpec(memory_space=pl.ANY),
-            pl.BlockSpec(memory_space=pltpu.VMEM),
-            pl.BlockSpec(memory_space=pltpu.VMEM),
+            pl.BlockSpec(memory_space=pl.ANY),
+            pl.BlockSpec(memory_space=pl.ANY),
+            pl.BlockSpec(memory_space=pl.ANY),
         ],
         out_specs=(pl.BlockSpec(memory_space=pl.ANY), pl.BlockSpec(memory_space=pltpu.VMEM)),
         scratch_shapes=[
             vmem(2, nf, 3, rows, NY), vmem(nf, 3, rows, NY), vmem(3, rows, NY),
             vmem(S, 2, 8, 512), vmem(S, 2, 8, 512),
             vmem(S, 2, nf * 3, NY), vmem(S, 2, nf * 3, NY),
-            vmem(S, 2, 48, NY), vmem(2, 2, 32, NY), vmem(S, 2, 32, NY),
+            vmem(S, 2, 32, NY), vmem(S, 2, 8, 512), vmem(S, 2, 8, 512),
+            vmem(2, 2, 32, NY), vmem(S, 2, 32, NY), vmem(2, rows, NY), pltpu.SMEM((nf,), jnp.int32),
             vmem(S, 2, rows, NY), vmem(S, 2, rows, NY), vmem(S, 2, rows, NY), vmem(S, 2, rows, NY),
             vmem(12, rows, NY), vmem(S, R, 8, 128),
-            dma((4,)), dma((nf,)),
-            dma((S, 2)), dma((S, 2)), dma((S, 2)), dma((S, 2)), dma((S, 2)), dma((S, 2)),
+            dma((4,)), dma((3,)), dma((nf,)),
+            *[dma((S, 2))] * 8,
             dma((S, K)), dma((S, K)), dma((S, K)), dma((S, K)),
             dma((S, 2, K)), dma((S, 2, K)), dma((S, R)), dma((S, R)),
         ],
         compiler_params=pltpu.CompilerParams(
-            collective_id=0, has_side_effects=True, vmem_limit_bytes=52 * 1024 * 1024
+            collective_id=0, has_side_effects=True, vmem_limit_bytes=63 * 1024 * 1024
         ),
     )(seeds, deviation, velocity, forcing)
 

time: 145 us -> 138 us (0.952)
  Pallas kernels: 135 us -> 130 us
  local copies, waits for them, and re-layouts: 9.54 us -> 7.03 us
    pallas_call x1, Pallas kernels: 135 us -> 130 us  [body(): pl.pallas_call(functools.partial(kernel, R, F), out_shape=(jax.ShapeDtype...]
    unnamed x8 -> x4, local copies, waits for them, and re-layouts: 9.54 us -> 7.03 us
where the time goes in v2:
time: 138 us
  Pallas kernels  130 us (94%)
  local copies, waits for them, and re-layouts  7.03 us (5%)
    pallas_call x1, Pallas kernels, body(): pl.pallas_call(functools.partial(kernel, R, F), out_shape=(jax.ShapeDtype...  130 us
    unnamed x4, local copies, waits for them, and re-layouts  7.03 us

profile of v2, /device:TPU:0, one launch (start us, length us, event | category | flops | bytes accessed | tf_op | source)
XLA Modules:
  0.0 138.1 jit_solution(16670132456428690963)
XLA Ops:
  0.6 130.4 %shard_map.59 = (f32[16,3,16,2048]{3,2,1,0:T(8,128)}, f32[2,16,2048]{2,1,0:T(8,128)}) custom-call(s32[16]{0:T(128)} %seeds_in.1, f32[16,3,16,2048]{3,2,1,0:T(8,128)} %dev.1, f32[2,16,2048]{2,1,0:T(8,128)} %vel.1, f32[2,16,2048]{2,1,0:T(8,128)} %frc.1), custom_call_target="tpu_custom_call" | custom-call | tf_op jit(solution)/shard_map/pallas_call | solution.py:440
  131.0 0.0 copy-start
  131.0 6.3 %copy.8 = f32[16,3,16,2048]{3,2,1,0:T(8,128)} copy(f32[16,3,16,2048]{3,2,1,0:T(8,128)} %get-tuple-element.4) | data formatting | bytes 12582912
  137.4 0.0 copy-done
  137.4 0.7 copy.9
Async XLA Ops:
  131.0 6.3 %copy-start = (f32[2,16,2048]{2,1,0:T(8,128)S(1)}, f32[2,16,2048]{2,1,0:T(8,128)}, u32[]{:S(2)}) copy-start(f32[2,16,2048]{2,1,0:T(8,128)} %get-tuple-element.5) | copy-start | bytes 786436

commit v3 on v2

--- a/solution.py
+++ b/solution.py
@@ -19,7 +19,7 @@
 SIGMA = 1.0
 
 K = 8
-LAG = 2
+LAG = 3
 MESH = pl.DeviceIdType.MESH
 
 
@@ -223,38 +223,47 @@
         lax.fori_loop(lo, hi, one, 0)
 
     def chain(step):
-        for i in range(K + LAG):
-            if i < K:
-                @pl.when(not_end)
-                def _():
-                    in_copy(step, i).wait_recv()
-                    at = slice(i * CW, i * CW + CW)
-                    FP[step, :, :, at] = FP[step, :, :, at] + CA[step, :, :, at]
-
-                @pl.when(is_mid)
-                def _():
+        def relay(i):
+            @pl.when(not_end)
+            def _():
+                in_copy(step, i).wait_recv()
+                at = slice(i * CW, i * CW + CW)
+                FP[step, :, :, at] = FP[step, :, :, at] + CA[step, :, :, at]
+
+        def spread(j, middle):
+            at = slice(j * CW, j * CW + CW)
+            mid_copy(step, j).wait_recv()
+            total = CB[step, :, :, at]
+            if middle:
+                total = FP[step, :, :, at] + total
+            TT[step, :, :, at] = total
+
+            @pl.when(not_end)
+            def _():
+                total_copy(step, j).start()
+
+            RH[step, :, 8:24, at] = FR[:, :, at] + total
+            rh_copy(step, 0, j).start()
+            rh_copy(step, 1, j).start()
+
+        @pl.when(is_mid)
+        def _():
+            for i in range(K + LAG):
+                if i < K:
+                    relay(i)
                     mid_copy(step, i).start()
-
-                @pl.when(jnp.logical_not(is_mid))
-                def _():
-                    in_copy(step, i).start()
-
-                noise(step, i * nf // 16, (i + 1) * nf // 16)
-            if i >= LAG:
-                j = i - LAG
-                at = slice(j * CW, j * CW + CW)
-                mid_copy(step, j).wait_recv()
-                got = CB[step, :, :, at]
-                total = jnp.where(is_mid, FP[step, :, :, at] + got, got)
-                TT[step, :, :, at] = total
-
-                @pl.when(not_end)
-                def _():
-                    total_copy(step, j).start()
-
-                RH[step, :, 8:24, at] = FR[:, :, at] + total
-                rh_copy(step, 0, j).start()
-                rh_copy(step, 1, j).start()
+                    noise(step, i * nf // 16, (i + 1) * nf // 16)
+                if i >= LAG:
+                    spread(i - LAG, True)
+
+        @pl.when(jnp.logical_not(is_mid))
+        def _():
+            for i in range(K):
+                relay(i)
+                in_copy(step, i).start()
+            noise(step, 0, nf // 2)
+            for j in range(K):
+                spread(j, False)
 
     factor = 1.0 / (ALPHA + 4.0)
 

time: 138 us -> 83.8 us (0.61)
  Pallas kernels: 130 us -> 75.9 us
    pallas_call x1, Pallas kernels: 130 us -> 75.9 us  [body(): pl.pallas_call(functools.partial(kernel, R, F), out_shape=(jax.ShapeDtype...]
where the time goes in v3:
time: 83.8 us; the launch traced here: 83.6 us
  Pallas kernels  75.9 us (91%)
  local copies, waits for them, and re-layouts  7.03 us (8%)
    pallas_call x1, Pallas kernels, body(): pl.pallas_call(functools.partial(kernel, R, F), out_shape=(jax.ShapeDtype...  75.9 us
    unnamed x4, local copies, waits for them, and re-layouts  7.03 us

profile of v3, /device:TPU:0, one launch (start us, length us, event | category | flops | bytes accessed | tf_op | source)
XLA Modules:
  0.0 83.6 jit_solution(14005318159524674063)
XLA Ops:
  0.6 75.9 %shard_map.59 = (f32[16,3,16,2048]{3,2,1,0:T(8,128)}, f32[2,16,2048]{2,1,0:T(8,128)}) custom-call(s32[16]{0:T(128)} %seeds_in.1, f32[16,3,16,2048]{3,2,1,0:T(8,128)} %dev.1, f32[2,16,2048]{2,1,0:T(8,128)} %vel.1, f32[2,16,2048]{2,1,0:T(8,128)} %frc.1), custom_call_target="tpu_custom_call" | custom-call | tf_op jit(solution)/shard_map/pallas_call | solution.py:449
  76.6 0.0 copy-start
  76.6 6.3 %copy.8 = f32[16,3,16,2048]{3,2,1,0:T(8,128)} copy(f32[16,3,16,2048]{3,2,1,0:T(8,128)} %get-tuple-element.4) | data formatting | bytes 12582912
  82.9 0.0 copy-done
  82.9 0.7 copy.9
Async XLA Ops:
  76.6 6.3 %copy-start = (f32[2,16,2048]{2,1,0:T(8,128)S(1)}, f32[2,16,2048]{2,1,0:T(8,128)}, u32[]{:S(2)}) copy-start(f32[2,16,2048]{2,1,0:T(8,128)} %get-tuple-element.5) | copy-start | bytes 786436

commit v4 on v3

--- a/solution.py
+++ b/solution.py
@@ -109,13 +109,13 @@
     def _():
         pl.semaphore_signal(barrier, inc=1, device_id=outward, device_id_type=MESH)
 
-    def ses_copy(step, side):
-        return remote(SES.at[step, side], SER.at[step, 1 - side], ses_s.at[step, side],
-                      ses_r.at[step, 1 - side], south if side == 0 else north)
-
-    def es_copy(step, side):
-        return remote(ES.at[step, side], ER.at[step, 1 - side], es_s.at[step, side],
-                      es_r.at[step, 1 - side], south if side == 0 else north)
+    def ses_copy(step, side, c):
+        return remote(SES.at[step, side, c], SER.at[step, 1 - side, c], ses_s.at[step, side, c],
+                      ses_r.at[step, 1 - side, c], south if side == 0 else north)
+
+    def es_copy(step, side, h):
+        return remote(ES.at[step, side, h], ER.at[step, 1 - side, h], es_s.at[step, side, h],
+                      es_r.at[step, 1 - side, h], south if side == 0 else north)
 
     def u_copy(step, side):
         src = U32.at[step, :, pl.ds(8 if side == 0 else 16, 8)]
@@ -162,29 +162,36 @@
         return remote(SPR.at[step, 0], SPR.at[step, p], sp_s.at[step, p], sp_r.at[step, p],
                       {"rows": lax.rem(r + p, R)})
 
-    def stress(step):
-        for c in range(NC):
-            if step == 0:
-                loads[c].wait()
-            at = slice(c * W, c * W + W)
-
-            def add(i, acc):
-                tensor = [D[step, i, m, :, at] for m in range(3)]
-                for m in range(3):
-                    ES[step, 0, pl.ds(3 * i + m, 1), at] = tensor[m][0:1]
-                    ES[step, 1, pl.ds(3 * i + m, 1), at] = tensor[m][15:16]
-                spring = (1.0 + 2.0 / LMAX2) + (tensor[0] + tensor[2]) * (1.0 / LMAX2)
-                return tuple(acc[m] + spring * tensor[m] for m in range(3))
-
-            zero = jnp.zeros((16, W), jnp.float32)
-            acc = lax.fori_loop(0, nf, add, (zero, zero, zero))
-            acc = [one * (G_COEF / FIELDS) for one in acc]
-            for m in range(3):
-                ST[m, :, at] = acc[m]
-            for m in (1, 2):
-                row = (m - 1) * NC + c
-                SES[step, 0, row:row + 1, :] = acc[m][0:1]
-                SES[step, 1, row:row + 1, :] = acc[m][15:16]
+    nh = nf // 2
+
+    def stress(step, c):
+        if step == 0:
+            loads[c].wait()
+        at = slice(c * W, c * W + W)
+        zero = jnp.zeros((16, W), jnp.float32)
+        acc = (zero, zero, zero)
+        for h in range(2):
+            def add(pair, acc):
+                for q in range(2):
+                    i = 2 * pair + q
+                    tensor = [D[step, h * nh + i, m, :, at] for m in range(3)]
+                    for m in range(3):
+                        ES[step, 0, h, pl.ds(3 * i + m, 1), at] = tensor[m][0:1]
+                        ES[step, 1, h, pl.ds(3 * i + m, 1), at] = tensor[m][15:16]
+                    spring = (1.0 + 2.0 / LMAX2) + (tensor[0] + tensor[2]) * (1.0 / LMAX2)
+                    acc = tuple(acc[m] + spring * tensor[m] for m in range(3))
+                return acc
+
+            acc = lax.fori_loop(0, nh // 2, add, acc)
+        acc = [one * (G_COEF / FIELDS) for one in acc]
+        for m in range(3):
+            ST[m, :, at] = acc[m]
+        for m in (1, 2):
+            rows = slice(4 * m - 4, 4 * m)
+            SES[step, 0, c, rows, :] = jnp.broadcast_to(acc[m][0:1], (4, W))
+            SES[step, 1, c, rows, :] = jnp.broadcast_to(acc[m][15:16], (4, W))
+        for side in range(2):
+            ses_copy(step, side, c).start()
 
     row16 = lax.broadcasted_iota(jnp.int32, (16, W), 0)
 
@@ -194,11 +201,20 @@
 
     def force(step, c):
         at = slice(c * W, c * W + W)
+        for side in range(2):
+            ses_copy(step, side, c).wait_recv()
         for comp in range(2):
             west, east = west_east(lambda lo, hi: ST[comp, :, lo:hi], c * W, W, NY)
-            row = comp * NC + c
-            down, up = with_edges(ST[comp + 1, :, at], SER[step, 0, row:row + 1, :], SER[step, 1, row:row + 1, :])
+            row = comp * 4
+            down, up = with_edges(
+                ST[comp + 1, :, at], SER[step, 0, c, row:row + 1, :], SER[step, 1, c, row:row + 1, :]
+            )
             FP[step, comp, :, at] = ((east - west) + (up - down)) * 0.5
+
+        @pl.when(jnp.logical_not(not_end))
+        def _():
+            for i in range(c * K // NC, (c + 1) * K // NC):
+                (mid_copy if F == 2 else in_copy)(step, i).start()
 
     iota_cells = lax.broadcasted_iota(jnp.int32, (16, W), 0) * NY + lax.broadcasted_iota(jnp.int32, (16, W), 1)
 
@@ -222,13 +238,16 @@
 
         lax.fori_loop(lo, hi, one, 0)
 
+    order = [(i + K // NC) % K for i in range(K)]
+
     def chain(step):
-        def relay(i):
+        def relay(i, copy):
             @pl.when(not_end)
             def _():
                 in_copy(step, i).wait_recv()
                 at = slice(i * CW, i * CW + CW)
                 FP[step, :, :, at] = FP[step, :, :, at] + CA[step, :, :, at]
+                copy(step, i).start()
 
         def spread(j, middle):
             at = slice(j * CW, j * CW + CW)
@@ -250,19 +269,17 @@
         def _():
             for i in range(K + LAG):
                 if i < K:
-                    relay(i)
-                    mid_copy(step, i).start()
+                    relay(order[i], mid_copy)
                     noise(step, i * nf // 16, (i + 1) * nf // 16)
                 if i >= LAG:
-                    spread(i - LAG, True)
+                    spread(order[i - LAG], True)
 
         @pl.when(jnp.logical_not(is_mid))
         def _():
-            for i in range(K):
-                relay(i)
-                in_copy(step, i).start()
+            for i in order:
+                relay(i, in_copy)
             noise(step, 0, nf // 2)
-            for j in range(K):
+            for j in order:
                 spread(j, False)
 
     factor = 1.0 / (ALPHA + 4.0)
@@ -342,11 +359,13 @@
     def store_out(i):
         return pltpu.make_async_copy(D.at[0, i], out_d.at[i], out_sem.at[i])
 
-    def advance(step, dt, loud):
+    def advance(step, dt, loud, h):
         pull = jnp.broadcast_to(dt * (1.0 / (LMAX2 * LAMBDA)), (16, 128))
         loud = jnp.broadcast_to(loud, (16, 128))
 
-        def one(i, _):
+        def one(k, _):
+            i = h * nh + k
+
             def walk(m):
                 return tiles_with_sides(lambda j: D[step, i, m, :, j * 128:j * 128 + 128], NT)
 
@@ -356,14 +375,14 @@
                 if j % 2 == 0:
                     pair = slice(j * 128, j * 128 + 256)
                     rims = [
-                        [ER[step, side, pl.ds(3 * i + m, 1), pair] for m in range(3)] for side in range(2)
+                        [ER[step, side, h, pl.ds(3 * k + m, 1), pair] for m in range(3)] for side in range(2)
                     ]
                 part = slice(j % 2 * 128, j % 2 * 128 + 128)
                 a, b, d = [one[1] for one in both]
                 q = (a + d) * pull
                 xb, yb = COEF[7, :, at] * b, COEF[8, :, at] * b
                 cross = (xb + xb, COEF[7, :, at] * d + COEF[8, :, at] * a, yb + yb)
-                cw, ce, cs, cn = [COEF[k, :, at] for k in range(4)]
+                cw, ce, cs, cn = [COEF[n, :, at] for n in range(4)]
                 for m, (_, x, west, east) in enumerate(both):
                     down, up = south_north(x)
                     down = jnp.where(row_a == 0, rims[0][m][:, part], down)
@@ -376,26 +395,27 @@
                 store_out(i).start()
             return 0
 
-        lax.fori_loop(0, nf, one, 0)
+        lax.fori_loop(0, nh, one, 0)
 
     for step in range(STEPS):
-        stress(step)
         if step == 0:
             pl.semaphore_wait(barrier, jnp.where(not_end, R + 1, R))
-        for side in range(2):
-            ses_copy(step, side).start()
+        for c in range(NC):
+            stress(step, c)
+            if c >= 2:
+                force(step, c - 1)
+        force(step, NC - 1)
+        force(step, 0)
         if step == 0:
             vel_load.wait()
             send_velocity(step)
             frc_load.wait()
             seed_load.wait()
         for side in range(2):
-            es_copy(step, side).start()
-        for side in range(2):
-            ses_copy(step, side).wait_recv()
-        for c in range(NC):
-            force(step, c)
+            es_copy(step, side, 0).start()
         chain(step)
+        for side in range(2):
+            es_copy(step, side, 1).start()
         noise(step, nf // 2, 3 * nf // 4)
         for side in range(2):
             u_copy(step, side).wait_recv()
@@ -411,16 +431,19 @@
             out_u[...] = UU[0, :, 8:24]
         noise(step, 3 * nf // 4, nf)
         dt, loud = coefficients(step)
-        for side in range(2):
-            es_copy(step, side).wait_recv()
-        advance(step, dt, loud)
+        for h in range(2):
+            for side in range(2):
+                es_copy(step, side, h).wait_recv()
+            advance(step, dt, loud, h)
 
     for step in range(STEPS):
         for side in range(2):
-            ses_copy(step, side).wait_send()
+            for c in range(NC):
+                ses_copy(step, side, c).wait_send()
             u_copy(step, side).wait_send()
             x_copy(step, side).wait_send()
-            es_copy(step, side).wait_send()
+            for h in range(2):
+                es_copy(step, side, h).wait_send()
         for c in range(K):
             in_copy(step, c).wait_send()
             rh_copy(step, 0, c).wait_send()
@@ -461,14 +484,14 @@
         out_specs=(pl.BlockSpec(memory_space=pl.ANY), pl.BlockSpec(memory_space=pltpu.VMEM)),
         scratch_shapes=[
             vmem(2, nf, 3, rows, NY), vmem(nf, 3, rows, NY), vmem(3, rows, NY),
-            vmem(S, 2, 8, 512), vmem(S, 2, 8, 512),
-            vmem(S, 2, nf * 3, NY), vmem(S, 2, nf * 3, NY),
+            vmem(S, 2, NY // 512, 8, 512), vmem(S, 2, NY // 512, 8, 512),
+            vmem(S, 2, 2, nf * 3 // 2, NY), vmem(S, 2, 2, nf * 3 // 2, NY),
             vmem(S, 2, 32, NY), vmem(S, 2, 8, 512), vmem(S, 2, 8, 512),
             vmem(2, 2, 32, NY), vmem(S, 2, 32, NY), vmem(2, rows, NY), pltpu.SMEM((nf,), jnp.int32),
             vmem(S, 2, rows, NY), vmem(S, 2, rows, NY), vmem(S, 2, rows, NY), vmem(S, 2, rows, NY),
             vmem(12, rows, NY), vmem(S, R, 8, 128),
             dma((4,)), dma((3,)), dma((nf,)),
-            *[dma((S, 2))] * 8,
+            *[dma((S, 2, NY // 512))] * 2, *[dma((S, 2))] * 4, *[dma((S, 2, 2))] * 2,
             dma((S, K)), dma((S, K)), dma((S, K)), dma((S, K)),
             dma((S, 2, K)), dma((S, 2, K)), dma((S, R)), dma((S, R)),
         ],

time: 83.8 us -> 83 us (level)
  no operation moved by 1% of the time
where the time goes in v4:
time: 83 us; the launch traced here: 82.9 us
  Pallas kernels  75.2 us (91%)
  local copies, waits for them, and re-layouts  7.03 us (8%)
    pallas_call x1, Pallas kernels, body(): pl.pallas_call(functools.partial(kernel, R, F), out_shape=(jax.ShapeDtype...  75.2 us
    unnamed x4, local copies, waits for them, and re-layouts  7.03 us

profile of v4, /device:TPU:0, one launch (start us, length us, event | category | flops | bytes accessed | tf_op | source)
XLA Modules:
  0.0 82.9 jit_solution(5336574955813213202)
XLA Ops:
  0.6 75.2 %shard_map.59 = (f32[16,3,16,2048]{3,2,1,0:T(8,128)}, f32[2,16,2048]{2,1,0:T(8,128)}) custom-call(s32[16]{0:T(128)} %seeds_in.1, f32[16,3,16,2048]{3,2,1,0:T(8,128)} %dev.1, f32[2,16,2048]{2,1,0:T(8,128)} %vel.1, f32[2,16,2048]{2,1,0:T(8,128)} %frc.1), custom_call_target="tpu_custom_call" | custom-call | tf_op jit(solution)/shard_map/pallas_call | solution.py:472
  75.8 0.0 copy-start
  75.8 6.3 %copy.8 = f32[16,3,16,2048]{3,2,1,0:T(8,128)} copy(f32[16,3,16,2048]{3,2,1,0:T(8,128)} %get-tuple-element.4) | data formatting | bytes 12582912
  82.2 0.0 copy-done
  82.2 0.7 copy.9
Async XLA Ops:
  75.8 6.3 %copy-start = (f32[2,16,2048]{2,1,0:T(8,128)S(1)}, f32[2,16,2048]{2,1,0:T(8,128)}, u32[]{:S(2)}) copy-start(f32[2,16,2048]{2,1,0:T(8,128)} %get-tuple-element.5) | copy-start | bytes 786436

commit v5 on v4

--- a/solution.py
+++ b/solution.py
@@ -59,7 +59,7 @@
 
 
 def kernel(
-    R, F, seeds_in, dev, vel, frc, out_d, out_u,
+    R, F, seeds_in, dev, vel, frc, out_d, out_u, out_root,
     D, NZ, ST, SES, SER, ES, ER, U32, XS, XR, UU, RH, FR, SD, FP, CA, CB, TT, COEF, SPR,
     in_sem, arg_sem, out_sem, ses_s, ses_r, u_s, u_r, x_s, x_r, es_s, es_r,
     in_s, a_r, b_r, t_s, rh_s, rh_r, sp_s, sp_r,
@@ -219,7 +219,7 @@
     iota_cells = lax.broadcasted_iota(jnp.int32, (16, W), 0) * NY + lax.broadcasted_iota(jnp.int32, (16, W), 1)
 
     def noise(step, lo, hi):
-        if hi <= lo:
+        if hi <= lo or step == STEPS - 1:
             return
 
         def one(i, _):
@@ -334,6 +334,9 @@
         dt = DT / (1.0 + top)
         loud = jnp.sqrt(dt) * (SIGMA / 18918.6)
         shift = loud * 32767.5
+        if step == STEPS - 1:
+            out_root[...] = jnp.broadcast_to(jnp.sqrt(dt) * SIGMA, (8, 128))
+            shift = 0.0
         for c in range(NC):
             at = slice(c * W, c * W + W)
             grads = []
@@ -390,7 +393,10 @@
                     fresh = (COEF[4 + m, :, at] - q) * x + cross[m]
                     fresh = fresh + (cw * west + ce * east)
                     fresh = fresh + (cs * down + cn * up)
-                    D[1 - step, i, m, :, at] = fresh + (COEF[9 + m, :, at] + loud * NZ[i, m, :, at])
+                    fixed = COEF[9 + m, :, at]
+                    if step < STEPS - 1:
+                        fixed = fixed + loud * NZ[i, m, :, at]
+                    D[1 - step, i, m, :, at] = fresh + fixed
             if step == STEPS - 1:
                 store_out(i).start()
             return 0
@@ -463,17 +469,31 @@
     lax.fori_loop(0, nf, finish, 0)
 
 
+def last_noise(seeds, shape):
+    iota = lambda dim: lax.broadcasted_iota(jnp.int32, shape, dim)
+    _, _, rows, NY = shape
+    h = (seeds * jnp.int32(2654435))[:, None, None, None] + (3 * (STEPS - 1) + iota(1)) * 97531
+    h = h + ((lax.axis_index("rows") * rows + iota(2)) * NY + iota(3))
+    h = jnp.bitwise_xor(h, lax.shift_right_logical(h, jnp.int32(16)))
+    h = h * jnp.int32(73244475)
+    h = jnp.bitwise_xor(h, lax.shift_right_logical(h, jnp.int32(16)))
+    h = h * jnp.int32(73244475)
+    h = jnp.bitwise_xor(h, lax.shift_right_logical(h, jnp.int32(16)))
+    return (jnp.bitwise_and(h, jnp.int32(65535)).astype(jnp.float32) - 32767.5) * (1.0 / 18918.6)
+
+
 def body(R, F, deviation, seeds, velocity, forcing):
     nf, _, rows, NY = deviation.shape
     f32 = jnp.float32
     S = STEPS
     dma = pltpu.SemaphoreType.DMA
     vmem = lambda *shape: pltpu.VMEM(shape, f32)
-    return pl.pallas_call(
+    fields, speed, root = pl.pallas_call(
         functools.partial(kernel, R, F),
         out_shape=(
             jax.ShapeDtypeStruct(deviation.shape, f32),
             jax.ShapeDtypeStruct(velocity.shape, f32),
+            jax.ShapeDtypeStruct((8, 128), f32),
         ),
         in_specs=[
             pl.BlockSpec(memory_space=pl.ANY),
@@ -481,7 +501,11 @@
             pl.BlockSpec(memory_space=pl.ANY),
             pl.BlockSpec(memory_space=pl.ANY),
         ],
-        out_specs=(pl.BlockSpec(memory_space=pl.ANY), pl.BlockSpec(memory_space=pltpu.VMEM)),
+        out_specs=(
+            pl.BlockSpec(memory_space=pl.ANY),
+            pl.BlockSpec(memory_space=pltpu.VMEM),
+            pl.BlockSpec(memory_space=pltpu.VMEM),
+        ),
         scratch_shapes=[
             vmem(2, nf, 3, rows, NY), vmem(nf, 3, rows, NY), vmem(3, rows, NY),
             vmem(S, 2, NY // 512, 8, 512), vmem(S, 2, NY // 512, 8, 512),
@@ -499,6 +523,7 @@
             collective_id=0, has_side_effects=True, vmem_limit_bytes=63 * 1024 * 1024
         ),
     )(seeds, deviation, velocity, forcing)
+    return fields + root[0, 0] * last_noise(seeds, deviation.shape), speed
 
 
 def solution(mesh):

time: 83 us -> 84.6 us (1.019)
  other arithmetic: 0 us -> 7.33 us
  local copies, waits for them, and re-layouts: 7.03 us -> 1.88 us
  Pallas kernels: 75.2 us -> 73.9 us
    add x0 -> x1, other arithmetic: none -> 6.66 us  [body(): return (fields + root[0, 0] * last_noise(seeds, deviation.shape), speed)]
    unnamed x4 -> x3, local copies, waits for them, and re-layouts: 7.03 us -> 0.71 us
    pallas_call x1, Pallas kernels: 75.2 us -> 73.9 us  [body(): pl.pallas_call(functools.partial(kernel, R, F), out_shape=(jax.ShapeDtype...]
    slice x0 -> x1, local copies, waits for them, and re-layouts: none -> 1.18 us  [body(): return (fields + root[0, 0] * last_noise(seeds, deviation.shape), speed)]
where the time goes in v5:
time: 84.6 us; the launch traced here: 84.5 us
  Pallas kernels  73.9 us (87%)
  other arithmetic  7.33 us (9%)
  local copies, waits for them, and re-layouts  1.88 us (2%)
  between operations  1.31 us (2%)
    pallas_call x1, Pallas kernels, body(): pl.pallas_call(functools.partial(kernel, R, F), out_shape=(jax.ShapeDtype...  73.9 us
    add x1, other arithmetic, body(): return (fields + root[0, 0] * last_noise(seeds, deviation.shape), speed)  6.66 us

profile of v5, /device:TPU:0, one launch (start us, length us, event | category | flops | bytes accessed | tf_op | source)
XLA Modules:
  0.0 84.5 jit_solution(5525232425628000319)
XLA Ops:
  0.6 0.7 add_multiply_fusion
  1.3 73.9 %shard_map.59 = (f32[16,3,16,2048]{3,2,1,0:T(8,128)}, f32[2,16,2048]{2,1,0:T(8,128)}, f32[8,128]{1,0:T(8,128)}) custom-call(s32[16]{0:T(128)} %seeds_in.1, f32[16,3,16,2048]{3,2,1,0:T(8,128)} %dev.1, f32[2,16,2048]{2,1,0:T(8,128)} %vel.1, f32[2,16,2048]{2,1,0:T(8,128)} %frc.1), custom_call_target="tpu_custom_call" | custom-call | tf_op jit(solution)/shard_map/pallas_call | solution.py:491
  75.3 1.2 %slice.3 = f32[1,1]{1,0:T(1,128)} slice(f32[8,128]{1,0:T(8,128)} %get-tuple-element.6), slice={[0:1], [0:1]} | slice | bytes 8 | tf_op jit(solution)/shard_map/slice | solution.py:526
  77.1 0.0 copy-start
  77.1 6.7 %fusion.6 = f32[16,3,16,2048]{3,2,1,0:T(8,128)} fusion(f32[16,3,16,2048]{3,2,1,0:T(8,128)} %get-tuple-element.5, f32[]{:T(128)} %bitcast, s32[16]{0:T(128)S(1)} %get-tuple-element.8, s32[3]{0:T(128)S(1)} %add_multiply_fusion.1, s32[16]{0:T(128)S(1)} %get-tuple-element.9), kind=kLoop, calls=%fused_computation.9 | loop fusion | flops 25165824 | bytes 12583056 | tf_op jit(solution)/shard_map/add | solution.py:526
  83.8 0.0 copy-done
  83.8 0.7 copy.7
  (1 shorter events, 0.0 us)
Async XLA Ops:
  77.1 6.7 %copy-start = (f32[2,16,2048]{2,1,0:T(8,128)S(1)}, f32[2,16,2048]{2,1,0:T(8,128)}, u32[]{:S(2)}) copy-start(f32[2,16,2048]{2,1,0:T(8,128)} %get-tuple-element.13) | copy-start | bytes 786436
